TPU v7x, 32 devices: a whole 2x2x4 slice. The times are simulated.
32 devices in a mesh: groups: 2 (over y), tm: 8 (over z, x), cells: 2 (over core).
Axes of the slice: x: 2, y: 2, z: 4, core: 2. Of those that a mesh axis runs over, the one named last changes fastest.
Arguments:
- propagator: bfloat16 [272, 48, 4, 256], P(('groups', 'tm'), None, None, 'cells'), parts along dimension 0, as said below
- tile_blocks: int32 [272, 2], P(('groups', 'tm')), parts along dimension 0, may hold values from 0 to 15, as said below
- histories: bfloat16 [16, 12, 48], P('tm'), may hold values from -6 to 6
Outputs:
- concentration: float32 [32, 12, 4, 256], P(('groups', 'tm'), None, None, 'cells'), parts along dimension 0
There are 2 independent parts, one for each index of `groups`. A program takes and returns all parts, laid end to end along the dimension named above; an argument that names none is the same for every part. Nothing has to cross between parts.
Inputs may be any that keep to these rules, and one draw needn't show every extreme that they name: `tile_blocks`: rows s * 17 to (s + 1) * 17 - 1 belong to two mirrored source blocks p and 15 - p, where p runs over a permutation of 0 to 7 from one such row group to the next; for each of the two source blocks every arrival block from it up to 15 appears in exactly one row, rows in any order. Tile n holds the propagator from source block tile_blocks[n, 0] to arrival block tile_blocks[n, 1].
All inputs are finite; a program needn't handle non-finite values.
Results may differ from a plain program's by a relative error of at most 0.0003.
Values may be sent and summed in bfloat16 or wider, within the bound.
A program may use at most 64 MiB of HBM per device.

v0:
```python
import jax
import jax.numpy as jnp
from jax import lax
from jax.sharding import PartitionSpec as P


def shards(propagator, tile_blocks, histories):
    all_histories = lax.all_gather(histories, "tm", axis=0, tiled=True)
    block_count = all_histories.shape[0]
    tracer_count = all_histories.shape[1]
    slot_count, source_width, months, cell_count = propagator.shape
    tile_rows = propagator.reshape(slot_count, source_width, months * cell_count)
    sources = tile_blocks[:, 0]
    arrivals = tile_blocks[:, 1]
    selector = (sources[:, None] == jnp.arange(block_count, dtype=jnp.int32)[None, :]).astype(
        jnp.bfloat16
    )
    chosen = jnp.dot(
        selector,
        all_histories.reshape(block_count, tracer_count * source_width),
        preferred_element_type=jnp.float32,
    )
    chosen = chosen.astype(jnp.bfloat16).reshape(slot_count, tracer_count, source_width)
    contribution = jnp.einsum("nrk,nkm->nrm", chosen, tile_rows, preferred_element_type=jnp.float32)
    partial_sums = (
        jnp.zeros((block_count, tracer_count, months * cell_count), jnp.float32)
        .at[arrivals]
        .add(contribution)
    )
    owned = lax.psum_scatter(partial_sums, "tm", scatter_dimension=0, tiled=True)
    return owned.reshape(owned.shape[0], tracer_count, months, cell_count)


def solution(mesh):
    in_specs = (
        P(("groups", "tm"), None, None, "cells"),
        P(("groups", "tm"), None),
        P("tm", None, None),
    )
    out_specs = P(("groups", "tm"), None, None, "cells")
    return jax.shard_map(shards, mesh=mesh, in_specs=in_specs, out_specs=out_specs, check_vma=False)
```

profile of v0, /device:TPU:0, one launch (start us, length us, event | category | flops | bytes accessed | tf_op | source)
XLA Modules:
  0.0 117.4 jit_solution(11963903710635323625)
XLA Ops:
  6.5 0.0 reduce-scatter.2.cloned.1.call-start
  6.5 0.8 slice_bitcast_fusion
  7.3 0.7 copy.9
  8.0 32.3 %all_gather.3 = bf16[16,12,48]{2,1,0:T(8,128)(2,1)S(1)} all-gather(bf16[2,12,48]{2,1,0:T(8,128)(2,1)S(1)} %copy.9), channel_id=1, replica_groups=mesh['groups'=2,'tm'=8,'cells'=2] {'tm'}, dimensions={0}, use_global_device_ids=true | all-gather | bytes 20736 | tf_op jit(solution)/shard_map/all_gather | solution.py:8
  40.3 0.1 reshape.12
  40.4 0.2 convolution_convert_fusion
  40.6 0.1 reshape.13
  40.7 1.7 %reshape.14 = bf16[17,48,512]{2,1,0:T(8,128)(2,1)S(1)} reshape(bf16[17,48,4,128]{3,2,1,0:T(4,128)(2,1)} %param.3) | data formatting | bytes 1671168 | tf_op jit(solution)/shard_map/reshape | solution.py:12
  42.4 0.2 fusion.2
  42.6 0.1 broadcast_in_dim.2
  42.7 2.1 %scatter_fusion = f32[16,12,512]{2,1,0:T(8,128)S(1)} fusion(f32[16,12,512]{2,1,0:T(8,128)S(1)} %broadcast_in_dim.2, s32[17]{0:T(128)S(1)} %get-tuple-element.6, f32[17,12,512]{2,1,0:T(8,128)S(1)} %fusion.2), kind=kCustom, calls=%fused_computation | custom fusion | flops 104448 | bytes 1253444 | tf_op jit(solution)/shard_map/scatter-add | solution.py:28
  44.8 0.0 copy-start
  44.8 0.8 copy-done
  45.6 0.0 reduce-scatter.2.cloned.1.call-update
  45.6 63.4 %reduce-scatter.2.cloned.1.call-done = f32[2,12,512]{2,1,0:T(8,128)} async-done(((f32[16,12,512]{2,1,0:T(8,128)}), f32[2,12,512]{2,1,0:T(8,128)}) %reduce-scatter.2.cloned.1.call-update) | async-done | bytes 49168 | tf_op jit(solution)/shard_map/reduce_scatter | solution.py:30
  109.0 1.5 %reshape.24 = f32[2,12,4,128]{3,2,1,0:T(4,128)} reshape(f32[2,12,512]{2,1,0:T(8,128)} %reduce-scatter.2.cloned.1.call-done) | data formatting | bytes 98304 | tf_op jit(solution)/shard_map/reshape | solution.py:31
Async XLA Ops:
  6.5 102.5 %reduce-scatter.2.cloned.1.call-start = ((), (), s32[]{:S(2)}) async-start(), calls=%async_computation.1 | async-start | bytes 589824 | tf_op jit(solution)/shard_map/reduce_scatter | solution.py:30
  44.8 0.8 copy-start
Sparse Core Ops, SparseCore 0:
  45.8 63.2 reduce-scatter.1
where the time goes:
time: 118 us; the launch traced here: 117 us
  waiting for transfers between devices  63.4 us (54%)
  blocking collectives  32.3 us (27%)
  between operations  13.4 us (11%)
  local copies, waits for them, and re-layouts  4.92 us (4%)
  other arithmetic  2.88 us (2%)
    reduce_scatter x1, waiting for transfers between devices, shards(): lax.psum_scatter(partial_sums, 'tm', scatter_dimension=0, tiled=True)  63.4 us
    all_gather x1, blocking collectives, shards(): all_histories = lax.all_gather(histories, 'tm', axis=0, tiled=True)  32.3 us
  transfers between devices with their start and end apart: 1, of which 1 were waited for; matrix products, arithmetic and copies ran while one was open for 0% of the time, Pallas kernels for 0%

commit v1 on v0

v1 whole, which is shorter than its diff:
```python
import functools

import jax
import jax.numpy as jnp
from jax import lax
from jax.experimental import pallas as pl
from jax.experimental.pallas import tpu as pltpu
from jax.sharding import PartitionSpec as P

MESH = pl.DeviceIdType.MESH
HALF = 64


def steps(low, high, body):
    if high - low <= 18:
        for index in range(low, high):
            body(index)
    else:
        lax.fori_loop(low, high, lambda index, carry: (body(index), carry)[1], 0)


def iota(shape, dim):
    return lax.broadcasted_iota(jnp.int32, shape, dim)


def one_hot(condition):
    return jnp.where(condition, 1.0, 0.0).astype(jnp.bfloat16)


def dot(a, b):
    return jnp.dot(a, b, preferred_element_type=jnp.float32)


def kernel(
    n, months, prop_hbm, blocks, hist, out,
    prop, message, held, expanded, parts, outgoing, incoming, first, second,
    prop_sem, hist_send, hist_recv, part_send, part_recv,
):
    me = lax.axis_index("tm")
    slots = prop.shape[0]
    count = 2 * n
    rows = out.shape[1]
    tracers = rows // months
    width = prop.shape[1]
    months_held = hist.shape[1]

    load = pltpu.make_async_copy(prop_hbm, prop, prop_sem)
    load.start()

    barrier = pltpu.get_barrier_semaphore()

    def greet(d):
        pl.semaphore_signal(
            barrier, inc=1, device_id={"tm": lax.rem(me + d, n)}, device_id_type=MESH
        )

    steps(1, n, greet)

    pick = iota((16, 2 * tracers), 1)
    row = iota((16, 2 * tracers), 0)
    to_lane = iota((months_held, 128), 1) - iota((months_held, 128), 0)
    packed = jnp.zeros((16, 128), jnp.float32)
    for j in range(2):
        block = dot(one_hot(pick == 2 * row + j), hist[...]).astype(jnp.bfloat16)
        packed += dot(block, one_hot(to_lane == j * HALF))
    message[...] = packed.astype(jnp.bfloat16)
    held[me] = message[...]

    pl.semaphore_wait(barrier, n - 1)

    def hist_copy(d):
        return pltpu.make_async_remote_copy(
            src_ref=message,
            dst_ref=held.at[me],
            send_sem=hist_send.at[d],
            recv_sem=hist_recv.at[d],
            device_id={"tm": lax.rem(me + d, n)},
            device_id_type=MESH,
        )

    steps(1, n, lambda d: hist_copy(d).start())

    parts[slots] = jnp.zeros((rows, 128), jnp.float32)

    def find(block):
        def look(slot, found):
            newest, older = found
            hit = blocks[1, slot] == block
            return jnp.where(hit, slot, newest), jnp.where(hit, newest, older)

        found = (jnp.int32(slots), jnp.int32(slots))
        if slots <= 18:
            for slot in range(slots):
                found = look(slot, found)
        else:
            found = lax.fori_loop(0, slots, look, found)
        first[block], second[block] = found

    steps(0, count, find)

    p = blocks[0, 0]
    q = count - 1 - p
    steps(1, n, lambda d: hist_copy(d).wait_recv())
    two = jnp.concatenate([held[p // 2], held[q // 2]], axis=0)
    wide = 2 * rows
    tall_row = iota((wide, 32), 0)
    late = jnp.where(tall_row >= rows, 1, 0)
    wanted = (tall_row - late * rows) // months + 16 * late
    tall = dot(one_hot(iota((wide, 32), 1) == wanted), two)
    side = jnp.where(iota((wide, 128), 0) >= rows, q % 2, p % 2)
    tall = jnp.where(iota((wide, 128), 1) // HALF == side, tall, 0.0).astype(jnp.bfloat16)
    spread = one_hot(iota((128, width), 0) % HALF == iota((128, width), 1) // months)
    full = dot(tall, spread)
    month = iota((wide, width), 0) % months == iota((wide, width), 1) % months
    full = jnp.where(month, full, 0.0).astype(jnp.bfloat16)
    expanded[0] = full[:rows]
    expanded[1] = full[rows:]

    load.wait()

    def multiply(slot):
        which = jnp.where(blocks[0, slot] == p, 0, 1)
        parts[slot] = dot(expanded[which], prop[slot])

    steps(0, slots, multiply)

    def partial(block):
        return parts[first[block]] + parts[second[block]]

    def part_copy(d):
        return pltpu.make_async_remote_copy(
            src_ref=outgoing.at[d],
            dst_ref=incoming.at[d],
            send_sem=part_send.at[d],
            recv_sem=part_recv.at[d],
            device_id={"tm": lax.rem(me + d, n)},
            device_id_type=MESH,
        )

    def send(d):
        to = lax.rem(me + d, n)
        for j in range(2):
            outgoing[d, j] = partial(2 * to + j)
        part_copy(d).start()

    steps(1, n, send)
    for j in range(2):
        out[j] = partial(2 * me + j)

    def receive(d):
        part_copy(d).wait_recv()
        out[...] += incoming[d]

    steps(1, n, receive)

    def drain(d):
        hist_copy(d).wait_send()
        part_copy(d).wait_send()

    steps(1, n, drain)


def solution(mesh):
    n = mesh.shape["tm"]

    def shards(propagator, tile_blocks, histories):
        slots, sources, months, cells = propagator.shape
        owned, tracers, _ = histories.shape
        rows = tracers * months
        width = sources * months
        out = pl.pallas_call(
            functools.partial(kernel, n, months),
            out_shape=jax.ShapeDtypeStruct((owned, rows, cells), jnp.float32),
            in_specs=[
                pl.BlockSpec(memory_space=pltpu.HBM),
                pl.BlockSpec(memory_space=pltpu.SMEM),
                pl.BlockSpec(memory_space=pltpu.VMEM),
            ],
            out_specs=pl.BlockSpec(memory_space=pltpu.VMEM),
            scratch_shapes=[
                pltpu.VMEM((slots, width, cells), jnp.bfloat16),
                pltpu.VMEM((16, 128), jnp.bfloat16),
                pltpu.VMEM((n, 16, 128), jnp.bfloat16),
                pltpu.VMEM((2, rows, width), jnp.bfloat16),
                pltpu.VMEM((slots + 1, rows, cells), jnp.float32),
                pltpu.VMEM((n, owned, rows, cells), jnp.float32),
                pltpu.VMEM((n, owned, rows, cells), jnp.float32),
                pltpu.SMEM((2 * n,), jnp.int32),
                pltpu.SMEM((2 * n,), jnp.int32),
                pltpu.SemaphoreType.DMA,
                pltpu.SemaphoreType.DMA((n,)),
                pltpu.SemaphoreType.DMA((n,)),
                pltpu.SemaphoreType.DMA((n,)),
                pltpu.SemaphoreType.DMA((n,)),
            ],
            compiler_params=pltpu.CompilerParams(
                collective_id=0, has_side_effects=True, vmem_limit_bytes=40 * 1024 * 1024
            ),
        )(
            propagator.reshape(slots, width, cells),
            tile_blocks.T,
            histories.transpose(1, 0, 2).reshape(owned * tracers, sources),
        )
        return out.reshape(owned, tracers, months, cells)

    in_specs = (
        P(("groups", "tm"), None, None, "cells"),
        P(("groups", "tm"), None),
        P("tm", None, None),
    )
    out_specs = P(("groups", "tm"), None, None, "cells")
    return jax.shard_map(shards, mesh=mesh, in_specs=in_specs, out_specs=out_specs, check_vma=False)
```

time: 118 us -> 22.6 us (0.19)
  waiting for transfers between devices: 63.4 us -> 0 us
  blocking collectives: 32.3 us -> 0 us
  Pallas kernels: 0 us -> 19.3 us
  between operations: 13.4 us -> 0.01 us
  other arithmetic: 2.88 us -> 0 us
  local copies, waits for them, and re-layouts: 4.92 us -> 3.14 us
    reduce_scatter x1 -> x0, waiting for transfers between devices: 63.4 us -> none  [shards(): lax.psum_scatter(partial_sums, 'tm', scatter_dimension=0, tiled=True)]
    all_gather x1 -> x0, blocking collectives: 32.3 us -> none  [shards(): all_histories = lax.all_gather(histories, 'tm', axis=0, tiled=True)]
    pallas_call x0 -> x1, Pallas kernels: none -> 19.3 us  [shards(): pl.pallas_call(functools.partial(kernel, n, months), out_shape=jax.ShapeD...]
    reshape x4 -> x0, local copies, waits for them, and re-layouts: 3.39 us -> none  [the longest x1 1.69 us: shards(): propagator.reshape(slot_count, source_width, months * cell_count)]
    scatter-add x1 -> x0, other arithmetic: 2.12 us -> none  [shards(): partial_sums = jnp.zeros((block_count, tracer_count, months * cell_count)...]
    unnamed x3 -> x7, local copies, waits for them, and re-layouts: 1.48 us -> 3.14 us
  transfers between devices with their start and end apart: 1 -> 0, of which waited for: 1 -> 0; matrix products, arithmetic and copies ran while one was open for 0% -> 0% of each run, Pallas kernels for 0% -> 0%
where the time goes in v1:
time: 22.6 us; the launch traced here: 22.4 us
  Pallas kernels  19.3 us (85%)
  local copies, waits for them, and re-layouts  3.14 us (14%)
    pallas_call x1, Pallas kernels, shards(): pl.pallas_call(functools.partial(kernel, n, months), out_shape=jax.ShapeD...  19.3 us
    unnamed x7, local copies, waits for them, and re-layouts  3.14 us

profile of v1, /device:TPU:0, one launch (start us, length us, event | category | flops | bytes accessed | tf_op | source)
XLA Modules:
  0.0 22.4 jit_solution(11563758084573759376)
XLA Ops:
  0.0 0.0 copy-start.2
  0.0 0.7 %copy-done.2 = s32[17,2]{0,1:T(2,128)S(1)} copy-done((s32[17,2]{0,1:T(2,128)S(1)}, s32[17,2]{0,1:T(2,128)}, u32[]{:S(2)}) %copy-start.2) | copy-done | bytes 160
  0.7 0.0 copy-start
  0.7 1.1 %copy-done = bf16[17,48,4,128]{3,2,1,0:T(4,128)(2,1)S(1)} copy-done((bf16[17,48,4,128]{3,2,1,0:T(4,128)(2,1)S(1)}, bf16[17,48,4,128]{3,2,1,0:T(4,128)(2,1)}, u32[]{:S(2)}) %copy-start) | copy-done | bytes 835608
  1.8 0.0 copy-start.1
  1.8 0.7 %copy-done.1 = bf16[2,12,48]{2,0,1:T(2,128)(2,1)S(1)} copy-done((bf16[2,12,48]{2,0,1:T(2,128)(2,1)S(1)}, bf16[2,12,48]{2,0,1:T(2,128)(2,1)}, u32[]{:S(2)}) %copy-start.1) | copy-done | bytes 2328
  2.5 19.3 %shard_map.37 = f32[2,48,128]{2,1,0:T(8,128)S(1)} custom-call(bf16[17,192,128]{2,1,0:T(8,128)(2,1)S(1)} %bitcast.6, s32[2,17]{1,0:T(2,128)S(1)} %bitcast.9, bf16[24,48]{1,0:T(8,128)(2,1)S(1)} %bitcast.8), custom_call_target="tpu_custom_call" | custom-call | tf_op jit(solution)/shard_map/pallas_call | solution.py:171
  21.8 0.6 %copy.5 = f32[2,12,4,128]{3,2,1,0:T(4,128)} copy(f32[2,12,4,128]{3,2,1,0:T(4,128)S(1)} %bitcast.7) | data formatting | bytes 98304
Async XLA Ops:
  0.0 0.7 %copy-start.2 = (s32[17,2]{0,1:T(2,128)S(1)}, s32[17,2]{0,1:T(2,128)}, u32[]{:S(2)}) copy-start(s32[17,2]{0,1:T(2,128)} %param.4) | copy-start | bytes 412
  0.7 1.1 %copy-start = (bf16[17,48,4,128]{3,2,1,0:T(4,128)(2,1)S(1)}, bf16[17,48,4,128]{3,2,1,0:T(4,128)(2,1)}, u32[]{:S(2)}) copy-start(bf16[17,48,4,128]{3,2,1,0:T(4,128)(2,1)} %param.3) | copy-start | bytes 2506756
  1.8 0.7 %copy-start.1 = (bf16[2,12,48]{2,0,1:T(2,128)(2,1)S(1)}, bf16[2,12,48]{2,0,1:T(2,128)(2,1)}, u32[]{:S(2)}) copy-start(bf16[2,12,48]{2,0,1:T(2,128)(2,1)} %param.5) | copy-start | bytes 6916

commit v2 on v1

--- a/solution.py
+++ b/solution.py
@@ -32,9 +32,9 @@
 
 
 def kernel(
-    n, months, prop_hbm, blocks, hist, out,
-    prop, message, held, expanded, parts, outgoing, incoming, first, second,
-    prop_sem, hist_send, hist_recv, part_send, part_recv,
+    n, months, prop_hbm, blocks_hbm, hist_hbm, out,
+    prop, blocks, hist, message, held, expanded, parts, outgoing, incoming, first, second,
+    prop_sem, blocks_sem, hist_sem, hist_send, hist_recv, part_send, part_recv,
 ):
     me = lax.axis_index("tm")
     slots = prop.shape[0]
@@ -44,6 +44,10 @@
     width = prop.shape[1]
     months_held = hist.shape[1]
 
+    load_hist = pltpu.make_async_copy(hist_hbm, hist, hist_sem)
+    load_hist.start()
+    load_blocks = pltpu.make_async_copy(blocks_hbm, blocks, blocks_sem)
+    load_blocks.start()
     load = pltpu.make_async_copy(prop_hbm, prop, prop_sem)
     load.start()
 
@@ -59,6 +63,7 @@
     pick = iota((16, 2 * tracers), 1)
     row = iota((16, 2 * tracers), 0)
     to_lane = iota((months_held, 128), 1) - iota((months_held, 128), 0)
+    load_hist.wait()
     packed = jnp.zeros((16, 128), jnp.float32)
     for j in range(2):
         block = dot(one_hot(pick == 2 * row + j), hist[...]).astype(jnp.bfloat16)
@@ -79,6 +84,8 @@
         )
 
     steps(1, n, lambda d: hist_copy(d).start())
+
+    load_blocks.wait()
 
     parts[slots] = jnp.zeros((rows, 128), jnp.float32)
 
@@ -173,12 +180,14 @@
             out_shape=jax.ShapeDtypeStruct((owned, rows, cells), jnp.float32),
             in_specs=[
                 pl.BlockSpec(memory_space=pltpu.HBM),
-                pl.BlockSpec(memory_space=pltpu.SMEM),
-                pl.BlockSpec(memory_space=pltpu.VMEM),
+                pl.BlockSpec(memory_space=pltpu.HBM),
+                pl.BlockSpec(memory_space=pltpu.HBM),
             ],
             out_specs=pl.BlockSpec(memory_space=pltpu.VMEM),
             scratch_shapes=[
                 pltpu.VMEM((slots, width, cells), jnp.bfloat16),
+                pltpu.SMEM((2, slots), jnp.int32),
+                pltpu.VMEM((owned * tracers, sources), jnp.bfloat16),
                 pltpu.VMEM((16, 128), jnp.bfloat16),
                 pltpu.VMEM((n, 16, 128), jnp.bfloat16),
                 pltpu.VMEM((2, rows, width), jnp.bfloat16),
@@ -188,13 +197,15 @@
                 pltpu.SMEM((2 * n,), jnp.int32),
                 pltpu.SMEM((2 * n,), jnp.int32),
                 pltpu.SemaphoreType.DMA,
+                pltpu.SemaphoreType.DMA,
+                pltpu.SemaphoreType.DMA,
                 pltpu.SemaphoreType.DMA((n,)),
                 pltpu.SemaphoreType.DMA((n,)),
                 pltpu.SemaphoreType.DMA((n,)),
                 pltpu.SemaphoreType.DMA((n,)),
             ],
             compiler_params=pltpu.CompilerParams(
-                collective_id=0, has_side_effects=True, vmem_limit_bytes=40 * 1024 * 1024
+                collective_id=0, has_side_effects=True, vmem_limit_bytes=63 * 1024 * 1024
             ),
         )(
             propagator.reshape(slots, width, cells),

time: 22.6 us -> 20.8 us (0.920)
  local copies, waits for them, and re-layouts: 3.14 us -> 1.42 us
    unnamed x7 -> x1, local copies, waits for them, and re-layouts: 3.14 us -> 1.42 us
where the time goes in v2:
time: 20.8 us; the launch traced here: 20.6 us
  Pallas kernels  19.2 us (92%)
  local copies, waits for them, and re-layouts  1.42 us (7%)
    pallas_call x1, Pallas kernels, shards(): pl.pallas_call(functools.partial(kernel, n, months), out_shape=jax.ShapeD...  19.2 us
    unnamed x1, local copies, waits for them, and re-layouts  1.42 us

profile of v2, /device:TPU:0, one launch (start us, length us, event | category | flops | bytes accessed | tf_op | source)
XLA Modules:
  0.0 20.6 jit_solution(5406414018847098787)
XLA Ops:
  0.0 19.2 %shard_map.37 = f32[2,48,128]{2,1,0:T(8,128)} custom-call(bf16[17,192,128]{2,1,0:T(8,128)(2,1)} %bitcast.6, s32[2,17]{1,0:T(2,128)} %bitcast.9, bf16[24,48]{1,0:T(8,128)(2,1)} %bitcast.8), custom_call_target="tpu_custom_call" | custom-call | tf_op jit(solution)/shard_map/pallas_call | solution.py:178
  19.2 1.4 %copy.5 = f32[2,12,4,128]{3,2,1,0:T(4,128)} copy(f32[2,12,4,128]{3,2,1,0:T(4,128)} %bitcast.7) | data formatting | bytes 98304

commit v3 on v2

--- a/solution.py
+++ b/solution.py
@@ -29,6 +29,23 @@
 
 def dot(a, b):
     return jnp.dot(a, b, preferred_element_type=jnp.float32)
+
+
+def encode(values):
+    groups = values.reshape(-1, 8, 128)
+    largest = jnp.max(jnp.abs(groups), axis=0)
+    exponent = jnp.floor(jnp.log2(jnp.maximum(largest, 1e-37)))
+    half = jnp.exp2(-0.5 * exponent)
+    scaled = groups * half * half * 16384.0
+    code = jnp.clip(jnp.floor(scaled + 0.5), -32767.0, 32767.0).astype(jnp.int32)
+    tail = jnp.concatenate([exponent, exponent], axis=0).astype(jnp.int32)
+    return code.reshape(-1, 128).astype(jnp.int16), tail.astype(jnp.int16)
+
+
+def decode(code, tail):
+    half = jnp.exp2(0.5 * tail.astype(jnp.int32).astype(jnp.float32)[:8])
+    groups = code.astype(jnp.int32).astype(jnp.float32).reshape(-1, 8, 128)
+    return (groups * (1.0 / 16384.0) * half * half).reshape(2, -1, 128)
 
 
 def kernel(
@@ -146,8 +163,10 @@
 
     def send(d):
         to = lax.rem(me + d, n)
-        for j in range(2):
-            outgoing[d, j] = partial(2 * to + j)
+        both = jnp.concatenate([partial(2 * to), partial(2 * to + 1)], axis=0)
+        code, tail = encode(both)
+        outgoing[d, : 2 * rows] = code
+        outgoing[d, 2 * rows :] = tail
         part_copy(d).start()
 
     steps(1, n, send)
@@ -156,7 +175,7 @@
 
     def receive(d):
         part_copy(d).wait_recv()
-        out[...] += incoming[d]
+        out[...] += decode(incoming[d, : 2 * rows], incoming[d, 2 * rows :])
 
     steps(1, n, receive)
 
@@ -192,8 +211,8 @@
                 pltpu.VMEM((n, 16, 128), jnp.bfloat16),
                 pltpu.VMEM((2, rows, width), jnp.bfloat16),
                 pltpu.VMEM((slots + 1, rows, cells), jnp.float32),
-                pltpu.VMEM((n, owned, rows, cells), jnp.float32),
-                pltpu.VMEM((n, owned, rows, cells), jnp.float32),
+                pltpu.VMEM((n, owned * rows + 16, cells), jnp.int16),
+                pltpu.VMEM((n, owned * rows + 16, cells), jnp.int16),
                 pltpu.SMEM((2 * n,), jnp.int32),
                 pltpu.SMEM((2 * n,), jnp.int32),
                 pltpu.SemaphoreType.DMA,

time: 20.8 us -> 17.9 us (0.86)
  Pallas kernels: 19.2 us -> 16.3 us
    pallas_call x1, Pallas kernels: 19.2 us -> 16.3 us  [shards(): pl.pallas_call(functools.partial(kernel, n, months), out_shape=jax.ShapeD...]
where the time goes in v3:
time: 17.9 us; the launch traced here: 17.7 us
  Pallas kernels  16.3 us (91%)
  local copies, waits for them, and re-layouts  1.42 us (8%)
    pallas_call x1, Pallas kernels, shards(): pl.pallas_call(functools.partial(kernel, n, months), out_shape=jax.ShapeD...  16.3 us
    unnamed x1, local copies, waits for them, and re-layouts  1.42 us

profile of v3, /device:TPU:0, one launch (start us, length us, event | category | flops | bytes accessed | tf_op | source)
XLA Modules:
  0.0 17.7 jit_solution(997662095165434354)
XLA Ops:
  0.0 16.3 %shard_map.37 = f32[2,48,128]{2,1,0:T(8,128)} custom-call(bf16[17,192,128]{2,1,0:T(8,128)(2,1)} %bitcast.6, s32[2,17]{1,0:T(2,128)} %bitcast.9, bf16[24,48]{1,0:T(8,128)(2,1)} %bitcast.8), custom_call_target="tpu_custom_call" | custom-call | tf_op jit(solution)/shard_map/pallas_call | solution.py:197
  16.3 1.4 %copy.5 = f32[2,12,4,128]{3,2,1,0:T(4,128)} copy(f32[2,12,4,128]{3,2,1,0:T(4,128)} %bitcast.7) | data formatting | bytes 98304

commit v4 on v3

--- a/solution.py
+++ b/solution.py
@@ -196,7 +196,7 @@
         width = sources * months
         out = pl.pallas_call(
             functools.partial(kernel, n, months),
-            out_shape=jax.ShapeDtypeStruct((owned, rows, cells), jnp.float32),
+            out_shape=pltpu.VMEM((owned, rows, cells), jnp.float32),
             in_specs=[
                 pl.BlockSpec(memory_space=pltpu.HBM),
                 pl.BlockSpec(memory_space=pltpu.HBM),

time: 17.9 us -> 16.5 us (0.922)
  local copies, waits for them, and re-layouts: 1.42 us -> 0.62 us
  Pallas kernels: 16.3 us -> 15.7 us
    unnamed x1, local copies, waits for them, and re-layouts: 1.42 us -> 0.62 us
    pallas_call x1, Pallas kernels: 16.3 us -> 15.7 us  [shards(): pl.pallas_call(functools.partial(kernel, n, months), out_shape=pltpu.VMEM...]
where the time goes in v4:
time: 16.5 us; the launch traced here: 16.3 us
  Pallas kernels  15.7 us (95%)
  local copies, waits for them, and re-layouts  0.62 us (4%)
    pallas_call x1, Pallas kernels, shards(): pl.pallas_call(functools.partial(kernel, n, months), out_shape=pltpu.VMEM...  15.7 us
    unnamed x1, local copies, waits for them, and re-layouts  0.62 us

profile of v4, /device:TPU:0, one launch (start us, length us, event | category | flops | bytes accessed | tf_op | source)
XLA Modules:
  0.0 16.3 jit_solution(1655913966446792697)
XLA Ops:
  0.0 15.7 %shard_map.37 = f32[2,48,128]{2,1,0:T(8,128)S(1)} custom-call(bf16[17,192,128]{2,1,0:T(8,128)(2,1)} %bitcast.7, s32[2,17]{1,0:T(2,128)} %bitcast.9, bf16[24,48]{1,0:T(8,128)(2,1)} %bitcast.8), custom_call_target="tpu_custom_call" | custom-call | tf_op jit(solution)/shard_map/pallas_call | solution.py:197
  15.7 0.6 %copy.5 = f32[2,12,4,128]{3,2,1,0:T(4,128)} copy(f32[2,12,4,128]{3,2,1,0:T(4,128)S(1)} %bitcast.6) | data formatting | bytes 98304

commit v5 on v2

--- a/solution.py
+++ b/solution.py
@@ -13,7 +13,7 @@
 
 def steps(low, high, body):
     if high - low <= 18:
-        for index in range(low, high):
+        for index in reversed(range(low, high)):
             body(index)
     else:
         lax.fori_loop(low, high, lambda index, carry: (body(index), carry)[1], 0)
@@ -29,6 +29,43 @@
 
 def dot(a, b):
     return jnp.dot(a, b, preferred_element_type=jnp.float32)
+
+
+def encode(values):
+    groups = values.reshape(-1, 8, 128)
+    largest = jnp.max(jnp.abs(groups), axis=0)
+    exponent = jnp.floor(jnp.log2(jnp.maximum(largest, 1e-37)))
+    half = jnp.exp2(-0.5 * exponent)
+    bits = exponent.astype(jnp.int32) + 128
+    coded = []
+    for i in range(groups.shape[0]):
+        scaled = groups[i] * half * half * 8192.0
+        code = jnp.clip(jnp.floor(scaled + 0.5), -16383.0, 16383.0).astype(jnp.int32) * 2
+        if i < 8:
+            code = code + ((bits >> i) & 1)
+        coded.append(code)
+    return jnp.concatenate(coded, axis=0).astype(jnp.int16)
+
+
+def decode(code):
+    groups = code.astype(jnp.int32).reshape(-1, 8, 128)
+    low = groups & 1
+    bits = low[0]
+    for i in range(1, 8):
+        bits = bits + (low[i] << i)
+    half = jnp.exp2(0.5 * (bits - 128).astype(jnp.float32))
+    values = (groups - low).astype(jnp.float32) * (1.0 / 16384.0) * half * half
+    return values.reshape(2, -1, 128)
+
+
+def partner(me, d, n):
+    if n & (n - 1):
+        return lax.rem(me + d, n)
+    other, bit = 0, 1
+    while bit < n:
+        other = other + bit * ((me // bit + d // bit) % 2)
+        bit *= 2
+    return other
 
 
 def kernel(
@@ -55,7 +92,7 @@
 
     def greet(d):
         pl.semaphore_signal(
-            barrier, inc=1, device_id={"tm": lax.rem(me + d, n)}, device_id_type=MESH
+            barrier, inc=1, device_id={"tm": partner(me, d, n)}, device_id_type=MESH
         )
 
     steps(1, n, greet)
@@ -79,7 +116,7 @@
             dst_ref=held.at[me],
             send_sem=hist_send.at[d],
             recv_sem=hist_recv.at[d],
-            device_id={"tm": lax.rem(me + d, n)},
+            device_id={"tm": partner(me, d, n)},
             device_id_type=MESH,
         )
 
@@ -140,14 +177,14 @@
             dst_ref=incoming.at[d],
             send_sem=part_send.at[d],
             recv_sem=part_recv.at[d],
-            device_id={"tm": lax.rem(me + d, n)},
+            device_id={"tm": partner(me, d, n)},
             device_id_type=MESH,
         )
 
     def send(d):
-        to = lax.rem(me + d, n)
-        for j in range(2):
-            outgoing[d, j] = partial(2 * to + j)
+        to = partner(me, d, n)
+        both = jnp.concatenate([partial(2 * to), partial(2 * to + 1)], axis=0)
+        outgoing[d] = encode(both)
         part_copy(d).start()
 
     steps(1, n, send)
@@ -156,7 +193,7 @@
 
     def receive(d):
         part_copy(d).wait_recv()
-        out[...] += incoming[d]
+        out[...] += decode(incoming[d])
 
     steps(1, n, receive)
 
@@ -177,7 +214,7 @@
         width = sources * months
         out = pl.pallas_call(
             functools.partial(kernel, n, months),
-            out_shape=jax.ShapeDtypeStruct((owned, rows, cells), jnp.float32),
+            out_shape=pltpu.VMEM((owned, rows, cells), jnp.float32),
             in_specs=[
                 pl.BlockSpec(memory_space=pltpu.HBM),
                 pl.BlockSpec(memory_space=pltpu.HBM),
@@ -192,8 +229,8 @@
                 pltpu.VMEM((n, 16, 128), jnp.bfloat16),
                 pltpu.VMEM((2, rows, width), jnp.bfloat16),
                 pltpu.VMEM((slots + 1, rows, cells), jnp.float32),
-                pltpu.VMEM((n, owned, rows, cells), jnp.float32),
-                pltpu.VMEM((n, owned, rows, cells), jnp.float32),
+                pltpu.VMEM((n, owned * rows, cells), jnp.int16),
+                pltpu.VMEM((n, owned * rows, cells), jnp.int16),
                 pltpu.SMEM((2 * n,), jnp.int32),
                 pltpu.SMEM((2 * n,), jnp.int32),
                 pltpu.SemaphoreType.DMA,

time: 20.8 us -> 16.4 us (0.79)
  Pallas kernels: 19.2 us -> 15.6 us
  local copies, waits for them, and re-layouts: 1.42 us -> 0.62 us
    pallas_call x1, Pallas kernels: 19.2 us -> 15.6 us  [shards(): pl.pallas_call(functools.partial(kernel, n, months), out_shape=pltpu.VMEM...]
    unnamed x1, local copies, waits for them, and re-layouts: 1.42 us -> 0.62 us
where the time goes in v5:
time: 16.4 us; the launch traced here: 16.2 us
  Pallas kernels  15.6 us (95%)
  local copies, waits for them, and re-layouts  0.62 us (4%)
    pallas_call x1, Pallas kernels, shards(): pl.pallas_call(functools.partial(kernel, n, months), out_shape=pltpu.VMEM...  15.6 us
    unnamed x1, local copies, waits for them, and re-layouts  0.62 us

profile of v5, /device:TPU:0, one launch (start us, length us, event | category | flops | bytes accessed | tf_op | source)
XLA Modules:
  0.0 16.2 jit_solution(5474040917653725392)
XLA Ops:
  0.0 15.6 %shard_map.37 = f32[2,48,128]{2,1,0:T(8,128)S(1)} custom-call(bf16[17,192,128]{2,1,0:T(8,128)(2,1)} %bitcast.7, s32[2,17]{1,0:T(2,128)} %bitcast.9, bf16[24,48]{1,0:T(8,128)(2,1)} %bitcast.8), custom_call_target="tpu_custom_call" | custom-call | tf_op jit(solution)/shard_map/pallas_call | solution.py:215
  15.6 0.6 %copy.5 = f32[2,12,4,128]{3,2,1,0:T(4,128)} copy(f32[2,12,4,128]{3,2,1,0:T(4,128)S(1)} %bitcast.6) | data formatting | bytes 98304

commit v6 on v5

--- a/solution.py
+++ b/solution.py
@@ -70,32 +70,32 @@
 
 def kernel(
     n, months, prop_hbm, blocks_hbm, hist_hbm, out,
-    prop, blocks, hist, message, held, expanded, parts, outgoing, incoming, first, second,
+    prop, blocks, hist, message, held, expanded, outgoing, incoming, first, second,
     prop_sem, blocks_sem, hist_sem, hist_send, hist_recv, part_send, part_recv,
 ):
     me = lax.axis_index("tm")
-    slots = prop.shape[0]
+    slots = blocks.shape[1]
     count = 2 * n
     rows = out.shape[1]
     tracers = rows // months
     width = prop.shape[1]
     months_held = hist.shape[1]
 
+    barrier = pltpu.get_barrier_semaphore()
+
+    def greet(d):
+        pl.semaphore_signal(
+            barrier, inc=1, device_id={"tm": partner(me, d, n)}, device_id_type=MESH
+        )
+
+    steps(1, n, greet)
+
     load_hist = pltpu.make_async_copy(hist_hbm, hist, hist_sem)
     load_hist.start()
     load_blocks = pltpu.make_async_copy(blocks_hbm, blocks, blocks_sem)
     load_blocks.start()
-    load = pltpu.make_async_copy(prop_hbm, prop, prop_sem)
+    load = pltpu.make_async_copy(prop_hbm, prop.at[:slots], prop_sem)
     load.start()
-
-    barrier = pltpu.get_barrier_semaphore()
-
-    def greet(d):
-        pl.semaphore_signal(
-            barrier, inc=1, device_id={"tm": partner(me, d, n)}, device_id_type=MESH
-        )
-
-    steps(1, n, greet)
 
     pick = iota((16, 2 * tracers), 1)
     row = iota((16, 2 * tracers), 0)
@@ -108,6 +108,15 @@
     message[...] = packed.astype(jnp.bfloat16)
     held[me] = message[...]
 
+    wide = 2 * rows
+    tall_row = iota((wide, 32), 0)
+    late = jnp.where(tall_row >= rows, 1, 0)
+    wanted = (tall_row - late * rows) // months + 16 * late
+    raise_rows = one_hot(iota((wide, 32), 1) == wanted)
+    spread = one_hot(iota((128, width), 0) % HALF == iota((128, width), 1) // months)
+    month = iota((rows, width), 0) % months == iota((rows, width), 1) % months
+    prop[slots] = jnp.zeros((width, 128), jnp.bfloat16)
+
     pl.semaphore_wait(barrier, n - 1)
 
     def hist_copy(d):
@@ -124,13 +133,18 @@
 
     load_blocks.wait()
 
-    parts[slots] = jnp.zeros((rows, 128), jnp.float32)
+    p = blocks[0, 0]
+    q = count - 1 - p
 
     def find(block):
         def look(slot, found):
-            newest, older = found
+            from_p, from_q = found
             hit = blocks[1, slot] == block
-            return jnp.where(hit, slot, newest), jnp.where(hit, newest, older)
+            is_p = blocks[0, slot] == p
+            return (
+                jnp.where(hit & is_p, slot, from_p),
+                jnp.where(hit & jnp.logical_not(is_p), slot, from_q),
+            )
 
         found = (jnp.int32(slots), jnp.int32(slots))
         if slots <= 18:
@@ -142,34 +156,20 @@
 
     steps(0, count, find)
 
-    p = blocks[0, 0]
-    q = count - 1 - p
+    side = jnp.where(iota((wide, 128), 0) >= rows, q % 2, p % 2)
+    keep = iota((wide, 128), 1) // HALF == side
     steps(1, n, lambda d: hist_copy(d).wait_recv())
     two = jnp.concatenate([held[p // 2], held[q // 2]], axis=0)
-    wide = 2 * rows
-    tall_row = iota((wide, 32), 0)
-    late = jnp.where(tall_row >= rows, 1, 0)
-    wanted = (tall_row - late * rows) // months + 16 * late
-    tall = dot(one_hot(iota((wide, 32), 1) == wanted), two)
-    side = jnp.where(iota((wide, 128), 0) >= rows, q % 2, p % 2)
-    tall = jnp.where(iota((wide, 128), 1) // HALF == side, tall, 0.0).astype(jnp.bfloat16)
-    spread = one_hot(iota((128, width), 0) % HALF == iota((128, width), 1) // months)
+    tall = jnp.where(keep, dot(raise_rows, two), 0.0).astype(jnp.bfloat16)
     full = dot(tall, spread)
-    month = iota((wide, width), 0) % months == iota((wide, width), 1) % months
-    full = jnp.where(month, full, 0.0).astype(jnp.bfloat16)
-    expanded[0] = full[:rows]
-    expanded[1] = full[rows:]
+    for j in range(2):
+        part = jnp.where(month, full[j * rows : (j + 1) * rows], 0.0)
+        expanded[j] = part.astype(jnp.bfloat16)
 
     load.wait()
 
-    def multiply(slot):
-        which = jnp.where(blocks[0, slot] == p, 0, 1)
-        parts[slot] = dot(expanded[which], prop[slot])
-
-    steps(0, slots, multiply)
-
     def partial(block):
-        return parts[first[block]] + parts[second[block]]
+        return dot(expanded[0], prop[first[block]]) + dot(expanded[1], prop[second[block]])
 
     def part_copy(d):
         return pltpu.make_async_remote_copy(
@@ -222,13 +222,12 @@
             ],
             out_specs=pl.BlockSpec(memory_space=pltpu.VMEM),
             scratch_shapes=[
-                pltpu.VMEM((slots, width, cells), jnp.bfloat16),
+                pltpu.VMEM((slots + 1, width, cells), jnp.bfloat16),
                 pltpu.SMEM((2, slots), jnp.int32),
                 pltpu.VMEM((owned * tracers, sources), jnp.bfloat16),
                 pltpu.VMEM((16, 128), jnp.bfloat16),
                 pltpu.VMEM((n, 16, 128), jnp.bfloat16),
                 pltpu.VMEM((2, rows, width), jnp.bfloat16),
-                pltpu.VMEM((slots + 1, rows, cells), jnp.float32),
                 pltpu.VMEM((n, owned * rows, cells), jnp.int16),
                 pltpu.VMEM((n, owned * rows, cells), jnp.int16),
                 pltpu.SMEM((2 * n,), jnp.int32),

time: 16.4 us -> 16.2 us (0.988)
  Pallas kernels: 15.6 us -> 15.4 us
    pallas_call x1, Pallas kernels: 15.6 us -> 15.4 us  [shards(): pl.pallas_call(functools.partial(kernel, n, months), out_shape=pltpu.VMEM...]
where the time goes in v6:
time: 16.2 us; the launch traced here: 16 us
  Pallas kernels  15.4 us (95%)
  local copies, waits for them, and re-layouts  0.62 us (4%)
    pallas_call x1, Pallas kernels, shards(): pl.pallas_call(functools.partial(kernel, n, months), out_shape=pltpu.VMEM...  15.4 us
    unnamed x1, local copies, waits for them, and re-layouts  0.62 us

profile of v6, /device:TPU:0, one launch (start us, length us, event | category | flops | bytes accessed | tf_op | source)
XLA Modules:
  0.0 16.0 jit_solution(3376054380593268133)
XLA Ops:
  0.0 15.4 %shard_map.37 = f32[2,48,128]{2,1,0:T(8,128)S(1)} custom-call(bf16[17,192,128]{2,1,0:T(8,128)(2,1)} %bitcast.7, s32[2,17]{1,0:T(2,128)} %bitcast.9, bf16[24,48]{1,0:T(8,128)(2,1)} %bitcast.8), custom_call_target="tpu_custom_call" | custom-call | tf_op jit(solution)/shard_map/pallas_call | solution.py:215
  15.4 0.6 %copy.5 = f32[2,12,4,128]{3,2,1,0:T(4,128)} copy(f32[2,12,4,128]{3,2,1,0:T(4,128)S(1)} %bitcast.6) | data formatting | bytes 98304

commit v7 on v6

--- a/solution.py
+++ b/solution.py
@@ -95,7 +95,6 @@
     load_blocks = pltpu.make_async_copy(blocks_hbm, blocks, blocks_sem)
     load_blocks.start()
     load = pltpu.make_async_copy(prop_hbm, prop.at[:slots], prop_sem)
-    load.start()
 
     pick = iota((16, 2 * tracers), 1)
     row = iota((16, 2 * tracers), 0)
@@ -130,6 +129,7 @@
         )
 
     steps(1, n, lambda d: hist_copy(d).start())
+    load.start()
 
     load_blocks.wait()
 
@@ -195,7 +195,7 @@
         part_copy(d).wait_recv()
         out[...] += decode(incoming[d])
 
-    steps(1, n, receive)
+    steps(1, n, lambda d: receive(n - d))
 
     def drain(d):
         hist_copy(d).wait_send()

time: 16.2 us -> 16.2 us (level)
  no operation moved by 1% of the time
where the time goes in v7:
time: 16.2 us; the launch traced here: 16 us
  Pallas kernels  15.4 us (95%)
  local copies, waits for them, and re-layouts  0.62 us (4%)
    pallas_call x1, Pallas kernels, shards(): pl.pallas_call(functools.partial(kernel, n, months), out_shape=pltpu.VMEM...  15.4 us
    unnamed x1, local copies, waits for them, and re-layouts  0.62 us

profile of v7, /device:TPU:0, one launch (start us, length us, event | category | flops | bytes accessed | tf_op | source)
XLA Modules:
  0.0 16.0 jit_solution(9422665101348880975)
XLA Ops:
  0.0 15.4 %shard_map.37 = f32[2,48,128]{2,1,0:T(8,128)S(1)} custom-call(bf16[17,192,128]{2,1,0:T(8,128)(2,1)} %bitcast.7, s32[2,17]{1,0:T(2,128)} %bitcast.9, bf16[24,48]{1,0:T(8,128)(2,1)} %bitcast.8), custom_call_target="tpu_custom_call" | custom-call | tf_op jit(solution)/shard_map/pallas_call | solution.py:215
  15.4 0.6 %copy.5 = f32[2,12,4,128]{3,2,1,0:T(4,128)} copy(f32[2,12,4,128]{3,2,1,0:T(4,128)S(1)} %bitcast.6) | data formatting | bytes 98304

commit v8 on v6

--- a/solution.py
+++ b/solution.py
@@ -70,7 +70,7 @@
 
 def kernel(
     n, months, prop_hbm, blocks_hbm, hist_hbm, out,
-    prop, blocks, hist, message, held, expanded, outgoing, incoming, first, second,
+    prop, blocks, hist, message, held, outgoing, incoming, first, second,
     prop_sem, blocks_sem, hist_sem, hist_send, hist_recv, part_send, part_recv,
 ):
     me = lax.axis_index("tm")
@@ -162,14 +162,15 @@
     two = jnp.concatenate([held[p // 2], held[q // 2]], axis=0)
     tall = jnp.where(keep, dot(raise_rows, two), 0.0).astype(jnp.bfloat16)
     full = dot(tall, spread)
+    sides = []
     for j in range(2):
         part = jnp.where(month, full[j * rows : (j + 1) * rows], 0.0)
-        expanded[j] = part.astype(jnp.bfloat16)
+        sides.append(part.astype(jnp.bfloat16))
 
     load.wait()
 
     def partial(block):
-        return dot(expanded[0], prop[first[block]]) + dot(expanded[1], prop[second[block]])
+        return dot(sides[0], prop[first[block]]) + dot(sides[1], prop[second[block]])
 
     def part_copy(d):
         return pltpu.make_async_remote_copy(
@@ -227,7 +228,6 @@
                 pltpu.VMEM((owned * tracers, sources), jnp.bfloat16),
                 pltpu.VMEM((16, 128), jnp.bfloat16),
                 pltpu.VMEM((n, 16, 128), jnp.bfloat16),
-                pltpu.VMEM((2, rows, width), jnp.bfloat16),
                 pltpu.VMEM((n, owned * rows, cells), jnp.int16),
                 pltpu.VMEM((n, owned * rows, cells), jnp.int16),
                 pltpu.SMEM((2 * n,), jnp.int32),

time: 16.2 us -> 16.2 us (level)
  no operation moved by 1% of the time
where the time goes in v8:
time: 16.2 us; the launch traced here: 16 us
  Pallas kernels  15.4 us (95%)
  local copies, waits for them, and re-layouts  0.62 us (4%)
    pallas_call x1, Pallas kernels, shards(): pl.pallas_call(functools.partial(kernel, n, months), out_shape=pltpu.VMEM...  15.4 us
    unnamed x1, local copies, waits for them, and re-layouts  0.62 us

profile of v8, /device:TPU:0, one launch (start us, length us, event | category | flops | bytes accessed | tf_op | source)
XLA Modules:
  0.0 16.0 jit_solution(14308751333772221012)
XLA Ops:
  0.0 15.4 %shard_map.37 = f32[2,48,128]{2,1,0:T(8,128)S(1)} custom-call(bf16[17,192,128]{2,1,0:T(8,128)(2,1)} %bitcast.7, s32[2,17]{1,0:T(2,128)} %bitcast.9, bf16[24,48]{1,0:T(8,128)(2,1)} %bitcast.8), custom_call_target="tpu_custom_call" | custom-call | tf_op jit(solution)/shard_map/pallas_call | solution.py:216
  15.4 0.6 %copy.5 = f32[2,12,4,128]{3,2,1,0:T(4,128)} copy(f32[2,12,4,128]{3,2,1,0:T(4,128)S(1)} %bitcast.6) | data formatting | bytes 98304
